TPU v7x, 256 devices: a whole 4x4x8 slice. The times are simulated.
256 devices in a mesh: chan: 32 (over z_lo, x, core), stn: 8 (over z_hi, y).
Axes of the slice: x: 4, y: 4, z: 8 (z_hi: 2, z_lo: 4; z = z_hi * 4 + z_lo), core: 2. Of those that a mesh axis runs over, the one named last changes fastest.
Arguments:
- samples: bfloat16 [2, 1024, 393216], P(None, 'stn', 'chan'), may hold values from -6 to 6
- chan_index: int32 [512], replicated, may hold values from 0 to 4095, as said below
- flags: int32 [512, 512], P('stn'), may hold values 0 or 1
Outputs:
- visibility: bfloat16 [512, 2, 1024, 640], P('chan', None, 'stn')
Inputs may be any that keep to these rules, and one draw needn't show every extreme that they name: `chan_index`: 512 distinct channel numbers; 0 and 4095 are among them.
All inputs are finite; a program needn't handle non-finite values. No bound on the sum of `flags` on one device may be relied on, other than what follows from the above.
Results may differ from a plain program's by a relative error of at most 0.0073.
Values may be sent and summed in bfloat16 or wider, within the bound.
A program may use at most 64 MiB of HBM per device.

v0:
```python
import math
import jax
import jax.numpy as jnp
from jax import lax
from jax.sharding import PartitionSpec as P

DFT_LEN = 4096
TAPS = 4


def from_behind(block, axis, distance):
    devices = range(lax.axis_size(axis))
    route = [(i - distance, i) for i in devices if i - distance in devices]
    return lax.ppermute(block, axis, route)


def window_table(tap_count, dft_length):
    sample_pos = jnp.arange(tap_count * dft_length, dtype=jnp.float32) + 0.5
    weights = jnp.sinc(sample_pos / dft_length - tap_count / 2.0)
    weights = weights * (0.5 - 0.5 * jnp.cos(2.0 * math.pi / (tap_count * dft_length) * sample_pos))
    weights = weights / jnp.sqrt(jnp.sum(weights * weights))
    return weights.reshape(tap_count, dft_length)


def dft_tables(chan_index, dft_length):
    row_index = jnp.arange(dft_length, dtype=jnp.int32)[:, None]
    phase_index = row_index * chan_index[None, :] % dft_length
    angles = phase_index.astype(jnp.float32) * (2.0 * math.pi / dft_length)
    return (jnp.cos(angles).astype(jnp.bfloat16), jnp.sin(angles).astype(jnp.bfloat16))


def transform(frames, cosine, sine_table):
    contract = (((0,), (3,)), ((), ()))
    along_cos = lax.dot_general(cosine, frames, contract, preferred_element_type=jnp.float32)
    along_sin = lax.dot_general(sine_table, frames, contract, preferred_element_type=jnp.float32)
    return jnp.stack(
        [along_cos[:, :, 0] + along_sin[:, :, 1], along_cos[:, :, 1] - along_sin[:, :, 0]], axis=2
    )


def carry_frames(tail_frames, window, lead_count):
    zero_frames = jnp.zeros_like(tail_frames)
    stretched = jnp.concatenate([tail_frames, zero_frames], axis=2)
    carried = jnp.zeros(tail_frames.shape, jnp.float32)
    for tap_index in range(lead_count):
        carried = (
            carried
            + stretched[:, :, tap_index : tap_index + lead_count, :].astype(jnp.float32)
            * window[tap_index]
        )
    return jnp.transpose(carried, (2, 0, 1, 3)).astype(jnp.bfloat16)


def on_device(samples, chan_index, flags):
    block_size = samples.shape[1]
    total_time = samples.shape[2]
    dft_length = DFT_LEN
    tap_count = TAPS
    lead_count = tap_count - 1
    spec_count = total_time // dft_length
    window = window_table(tap_count, dft_length)
    cosine, sine_table = dft_tables(chan_index, dft_length)
    own_frames = samples.reshape(2, block_size, spec_count, dft_length)
    local_pad = jnp.concatenate(
        [jnp.zeros((2, block_size, lead_count, dft_length), samples.dtype), own_frames], axis=2
    )
    current = jnp.zeros((2, block_size, spec_count, dft_length), jnp.float32)
    for tap_index in range(tap_count):
        current = (
            current
            + local_pad[:, :, tap_index : tap_index + spec_count, :].astype(jnp.float32)
            * window[tap_index]
        )
    current = jnp.transpose(current, (2, 0, 1, 3)).astype(jnp.bfloat16)
    main_part = transform(current, cosine, sine_table)
    received = from_behind(own_frames, "chan", 1)
    extra_part = transform(carry_frames(received, window, lead_count), cosine, sine_table)
    spectra = jnp.concatenate([main_part + extra_part, main_part[:, lead_count:]], axis=1)
    spectra = spectra.astype(jnp.bfloat16)
    turned = lax.all_to_all(spectra, "chan", split_axis=0, concat_axis=1, tiled=True)
    num_blocks = lax.axis_size("stn")
    own_index = lax.axis_index("stn")
    col_count = num_blocks // 2 + 1
    everyone = lax.all_gather(turned, "stn", axis=3, tiled=True)
    pieces = [
        lax.dynamic_slice_in_dim(
            everyone, (own_index - offset + num_blocks) % num_blocks * block_size, block_size, 3
        )
        for offset in range(col_count)
    ]
    columns = jnp.concatenate(pieces, axis=3)
    swapped = jnp.stack([turned[:, :, 1], -turned[:, :, 0]], axis=2)
    real_part = jnp.einsum("ctra,ctrb->cab", turned, columns, preferred_element_type=jnp.float32)
    imag_part = jnp.einsum("ctra,ctrb->cab", swapped, columns, preferred_element_type=jnp.float32)
    half_block = block_size // 2
    strips = [
        lax.dynamic_slice_in_dim(
            flags, (own_index - offset + num_blocks) % num_blocks * half_block, half_block, 1
        )
        for offset in range(col_count)
    ]
    keep_mask = (1 - jnp.concatenate(strips, axis=1)).astype(jnp.float32)
    keep_mask = jnp.repeat(jnp.repeat(keep_mask, 2, axis=0), 2, axis=1)
    total_spectra = turned.shape[1]
    visibility = jnp.stack([real_part, imag_part], axis=1) * keep_mask / total_spectra
    return visibility.astype(jnp.bfloat16)


def solution(mesh):
    in_specs = (P(None, "stn", "chan"), P(), P("stn", None))
    out_specs = P("chan", None, "stn", None)
    return jax.shard_map(
        on_device, mesh=mesh, in_specs=in_specs, out_specs=out_specs, check_vma=False
    )
```

profile of v0, /device:TPU:2, one launch (start us, length us, event | category | flops | bytes accessed | tf_op | source)
XLA Modules:
  0.0 375.2 jit_solution(14467493434903345234)
XLA Ops:
  6.5 8.6 %copy.35 = bf16[2,128,12288]{1,2,0:T(8,128)(2,1)} copy(bf16[2,128,12288]{2,1,0:T(8,128)(2,1)} %param.3) | data formatting | bytes 12582912 | tf_op args[0]
  15.2 1.9 collective-permute-start
  17.1 0.9 multiply_reduce_fusion
  18.7 0.3 broadcast_divide_fusion
  19.1 32.0 %fusion.69 = bf16[4096,512,1,1]{0,1,3,2:T(8,128)(2,1)S(1)} fusion(s32[512]{0:T(512)S(1)} %copy-done.1), kind=kLoop, calls=%fused_computation.31.clone.clone.1 | loop fusion | flops 31457280 | bytes 4196352 | tf_op jit(solution)/shard_map/dot_general | solution.py:35
  51.1 31.7 %fusion.71 = bf16[4096,512,1,1]{0,1,3,2:T(8,128)(2,1)S(1)} fusion(s32[512]{0:T(512)S(1)} %copy-done.1), kind=kLoop, calls=%fused_computation.30.clone.clone.1 | loop fusion | flops 31457280 | bytes 4196352 | tf_op jit(solution)/shard_map/dot_general | solution.py:34
  82.8 32.0 %fusion.73 = bf16[4096,512,1,1]{0,1,3,2:T(8,128)(2,1)S(1)} fusion(s32[512]{0:T(512)S(1)} %copy-done.1), kind=kLoop, calls=%fused_computation.31.clone.1.clone | loop fusion | flops 31457280 | bytes 4196352 | tf_op jit(solution)/shard_map/dot_general | solution.py:35
  114.8 31.7 %fusion.75 = bf16[4096,512,1,1]{0,1,3,2:T(8,128)(2,1)S(1)} fusion(s32[512]{0:T(512)S(1)} %copy-done.1), kind=kLoop, calls=%fused_computation.30.clone.1.clone | loop fusion | flops 31457280 | bytes 4196352 | tf_op jit(solution)/shard_map/dot_general | solution.py:34
  146.6 9.2 %fusion.9 = (bf16[3,2,128,4096]{2,3,0,1:T(8,128)(2,1)S(1)}, bf16[3,2,128,4096]{2,3,0,1:T(8,128)(2,1)S(1)}) fusion(bf16[2,128,3,4096]{1,3,2,0:T(8,128)(2,1)} %collective-permute-done, f32[4096]{0:T(1024)S(1)} %get-tuple-element.16, f32[4096]{0:T(1024)S(1)} %get-tuple-element.19, f32[4096]{0:T(1024)S(1)} %get-tuple-element.20, f32[4096]{0:T(1024)S(1)} %get-tuple-element.18, ...), kind=kLoop, calls=%fused_computation.21 | loop fusion | flops 59768832 | bytes 25247744 | tf_op jit(solution)/shard_map/convert_element_type | solution.py:51
  155.9 3.4 fusion.10
  159.3 3.4 fusion.12
  162.7 3.4 fusion.14
  166.1 3.4 fusion.16
  169.6 0.3 slice_add_fusion
  169.9 0.2 fusion.24
  170.1 0.8 copy.40
  170.9 30.1 %all_to_all.18 = bf16[512,3,2,128]{3,2,1,0:T(2,128)(2,1)S(1)} all-to-all(bf16[512,3,2,128]{3,2,1,0:T(2,128)(2,1)S(1)} %copy.40), channel_id=1, replica_groups=mesh['chan'=32,'stn'=8] {'chan'}, dimensions={0} | all-to-all | bytes 1572864 | tf_op jit(solution)/shard_map/all_to_all | solution.py:80
  201.1 0.1 copy.42
  201.2 1.2 copy.44
  202.9 0.1 reshape.22
  203.3 0.2 copy.48
  203.4 1.2 fusion.59
  204.7 145.4 %all-gather.2.cloned.1.call-done = bf16[16,96,2,1024]{3,1,2,0:T(8,128)(2,1)} async-done(((bf16[16,96,2,128]{3,1,2,0:T(8,128)(2,1)}), bf16[16,96,2,1024]{3,1,2,0:T(8,128)(2,1)}) %all-gather.2.cloned.1.call-update) | async-done | bytes 6291472 | tf_op jit(solution)/shard_map/all_gather | solution.py:84
  350.0 1.3 dynamic-slice_dynamic-update-slice_fusion.4
  351.3 1.3 dynamic-slice_dynamic-update-slice_fusion.3
  352.6 1.3 dynamic-slice_dynamic-update-slice_fusion.2
  354.0 1.3 dynamic-slice_dynamic-update-slice_fusion.1
  355.3 1.3 dynamic-slice_dynamic-update-slice_fusion
  356.6 1.2 convolution_bitcast_fusion.1
  357.9 1.1 convolution_bitcast_fusion
  359.0 3.8 %fusion.1 = bf16[16,2,128,640]{3,2,0,1:T(8,128)(2,1)} fusion(f32[16,1,128,640]{3,2,0,1:T(8,128)S(1)} %convolution_bitcast_fusion, f32[16,1,128,640]{3,2,0,1:T(8,128)S(1)} %convolution_bitcast_fusion.1, f32[128,640]{1,0:T(8,128)S(1)} %copy.48), kind=kLoop, calls=%fused_computation.11 | loop fusion | flops 10485760 | bytes 16056320 | tf_op jit(solution)/shard_map/convert_element_type | solution.py:106
  362.7 5.6 %copy.49 = bf16[16,2,128,640]{3,2,1,0:T(8,128)(2,1)} copy(bf16[16,2,128,640]{3,2,0,1:T(8,128)(2,1)} %fusion.1) | data formatting | bytes 10485760 | tf_op jit(solution)/shard_map/convert_element_type | solution.py:106
  (20 shorter events, 0.7 us)
Async XLA Ops:
  6.5 12.5 %copy-start.1 = (s32[512]{0:T(512)S(1)}, s32[512]{0:T(512)}, u32[]{:S(2)}) copy-start(s32[512]{0:T(512)} %param.4) | copy-start | bytes 6148
  6.5 343.5 %all-gather.2.cloned.1.call-start = ((), (), s32[]{:S(2)}) async-start(), calls=%async_computation.1 | async-start | bytes 7077888 | tf_op jit(solution)/shard_map/all_gather | solution.py:84
  15.2 131.4 %collective-permute-start = (bf16[2,128,3,4096]{1,3,2,0:T(8,128)(2,1)}, bf16[2,128,3,4096]{1,3,2,0:T(8,128)(2,1)}, u32[]{:S(2)}, u32[]{:S(2)}) collective-permute-start(bf16[2,128,3,4096]{1,3,2,0:T(8,128)(2,1)} %bitcast.44), channel_id=1, source_target_pairs={{0,8},{8,16},{16,24},{24,32},{32,40},{40,48},{48,56},{56,64},{64,7... | collective-permute-start | bytes 18874376 | tf_op jit(solution)/shard_map/ppermute | solution.py:14
  51.1 95.5 %slice-start = ((s8[6291456]{0:T(1024)(128)(4,1)}), s8[4194304]{0:T(1024)(128)(4,1)S(1)}, s32[]{:S(2)}) async-start(s8[6291456]{0:T(1024)(128)(4,1)} %bitcast.45), calls=%async_computation.2 | async-start | bytes 8388608
  82.8 63.8 %slice-start.1 = ((s8[6291456]{0:T(1024)(128)(4,1)}), s8[2097152]{0:T(1024)(128)(4,1)S(1)}, s32[]{:S(2)}) async-start(s8[6291456]{0:T(1024)(128)(4,1)} %bitcast.45), calls=%async_computation.3 | async-start | bytes 4194304
  169.9 32.6 %copy-start = (s32[64,512]{1,0:T(8,128)S(1)}, s32[64,512]{1,0:T(8,128)}, u32[]{:S(2)}) copy-start(s32[64,512]{1,0:T(8,128)} %param.5) | copy-start | bytes 393220
Sparse Core Ops, SparseCore 0:
  202.6 147.4 all-gather.1
where the time goes:
time: 376 us; the launch traced here: 375 us
  waiting for transfers between devices  145 us (39%)
  other arithmetic  143 us (38%)
  blocking collectives  30.1 us (8%)
  local copies, waits for them, and re-layouts  23.9 us (6%)
  matrix products  16 us (4%)
  between operations  14.5 us (4%)
    all_gather x1, waiting for transfers between devices, on_device(): everyone = lax.all_gather(turned, 'stn', axis=3, tiled=True)  145 us
    dot_general x2, other arithmetic, transform(): lax.dot_general(sine_table, frames, contract, preferred_element_type=jnp....  64 us
    dot_general x2, other arithmetic, transform(): lax.dot_general(cosine, frames, contract, preferred_element_type=jnp.floa...  63.4 us
    all_to_all x1, blocking collectives, on_device(): lax.all_to_all(spectra, 'chan', split_axis=0, concat_axis=1, tiled=True)  30.1 us
    unnamed x13, local copies, waits for them, and re-layouts  13.9 us
    convert_element_type x1, other arithmetic, carry_frames(): return jnp.transpose(carried, (2, 0, 1, 3)).astype(jnp.bfloat16)  9.25 us
  transfers between devices with their start and end apart: 2, of which 1 were waited for; matrix products, arithmetic and copies ran while one was open for 35% of the time, Pallas kernels for 0%

commit v1 on v0

--- a/solution.py
+++ b/solution.py
@@ -77,7 +77,9 @@
     extra_part = transform(carry_frames(received, window, lead_count), cosine, sine_table)
     spectra = jnp.concatenate([main_part + extra_part, main_part[:, lead_count:]], axis=1)
     spectra = spectra.astype(jnp.bfloat16)
-    turned = lax.all_to_all(spectra, "chan", split_axis=0, concat_axis=1, tiled=True)
+    turned = jnp.concatenate(
+        lax.all_to_all(jnp.stack(jnp.split(spectra, lax.axis_size("chan"), 0), 0), "chan", 0, 0), 1
+    )
     num_blocks = lax.axis_size("stn")
     own_index = lax.axis_index("stn")
     col_count = num_blocks // 2 + 1

time: 376 us -> 375 us (level)
    unnamed x13 -> x44, local copies, waits for them, and re-layouts: 13.9 us -> 14.3 us
where the time goes in v1:
time: 375 us
  waiting for transfers between devices  145 us (39%)
  other arithmetic  143 us (38%)
  blocking collectives  30.1 us (8%)
  local copies, waits for them, and re-layouts  23.2 us (6%)
  matrix products  16 us (4%)
  between operations  14.7 us (4%)
    all_gather x1, waiting for transfers between devices, on_device(): everyone = lax.all_gather(turned, 'stn', axis=3, tiled=True)  145 us
    dot_general x2, other arithmetic, transform(): lax.dot_general(sine_table, frames, contract, preferred_element_type=jnp....  64 us
    dot_general x2, other arithmetic, transform(): lax.dot_general(cosine, frames, contract, preferred_element_type=jnp.floa...  63.4 us
    all_to_all x1, blocking collectives, on_device(): lax.all_to_all(jnp.stack(jnp.split(spectra, lax.axis_size('chan'), 0), 0)...  30.1 us
    unnamed x44, local copies, waits for them, and re-layouts  14.3 us
    convert_element_type x1, other arithmetic, carry_frames(): return jnp.transpose(carried, (2, 0, 1, 3)).astype(jnp.bfloat16)  9.25 us
  transfers between devices with their start and end apart: 2, of which 1 were waited for; matrix products, arithmetic and copies ran while one was open for 35% of the time, Pallas kernels for 0%

profile of v1, /device:TPU:2, one launch (start us, length us, event | category | flops | bytes accessed | tf_op | source)
XLA Modules:
  0.0 374.7 jit_solution(9373891581062422651)
XLA Ops:
  6.5 8.6 %copy.12 = bf16[2,128,12288]{1,2,0:T(8,128)(2,1)} copy(bf16[2,128,12288]{2,1,0:T(8,128)(2,1)} %param.3) | data formatting | bytes 12582912 | tf_op args[0]
  15.2 1.9 collective-permute-start
  17.1 0.9 multiply_reduce_fusion
  18.7 0.3 broadcast_divide_fusion
  19.1 32.0 %fusion.69 = bf16[4096,512,1,1]{0,1,3,2:T(8,128)(2,1)S(1)} fusion(s32[512]{0:T(512)S(1)} %copy-done.1), kind=kLoop, calls=%fused_computation.31.clone.clone.1 | loop fusion | flops 31457280 | bytes 4196352 | tf_op jit(solution)/shard_map/dot_general | solution.py:35
  51.1 31.7 %fusion.71 = bf16[4096,512,1,1]{0,1,3,2:T(8,128)(2,1)S(1)} fusion(s32[512]{0:T(512)S(1)} %copy-done.1), kind=kLoop, calls=%fused_computation.30.clone.clone.1 | loop fusion | flops 31457280 | bytes 4196352 | tf_op jit(solution)/shard_map/dot_general | solution.py:34
  82.8 32.0 %fusion.73 = bf16[4096,512,1,1]{0,1,3,2:T(8,128)(2,1)S(1)} fusion(s32[512]{0:T(512)S(1)} %copy-done.1), kind=kLoop, calls=%fused_computation.31.clone.1.clone | loop fusion | flops 31457280 | bytes 4196352 | tf_op jit(solution)/shard_map/dot_general | solution.py:35
  114.8 31.7 %fusion.75 = bf16[4096,512,1,1]{0,1,3,2:T(8,128)(2,1)S(1)} fusion(s32[512]{0:T(512)S(1)} %copy-done.1), kind=kLoop, calls=%fused_computation.30.clone.1.clone | loop fusion | flops 31457280 | bytes 4196352 | tf_op jit(solution)/shard_map/dot_general | solution.py:34
  146.6 9.2 %fusion.9 = (bf16[3,2,128,4096]{2,3,0,1:T(8,128)(2,1)S(1)}, bf16[3,2,128,4096]{2,3,0,1:T(8,128)(2,1)S(1)}) fusion(bf16[2,128,3,4096]{1,3,2,0:T(8,128)(2,1)} %collective-permute-done, f32[4096]{0:T(1024)S(1)} %get-tuple-element.16, f32[4096]{0:T(1024)S(1)} %get-tuple-element.19, f32[4096]{0:T(1024)S(1)} %get-tuple-element.20, f32[4096]{0:T(1024)S(1)} %get-tuple-element.18, ...), kind=kLoop, calls=%fused_computation.21 | loop fusion | flops 59768832 | bytes 25247744 | tf_op jit(solution)/shard_map/convert_element_type | solution.py:51
  155.9 3.4 fusion.10
  159.3 3.4 fusion.12
  162.7 3.4 fusion.14
  166.1 3.4 fusion.16
  169.6 0.3 slice_add_fusion
  169.9 0.2 fusion.24
  170.6 30.1 %all_to_all.5 = bf16[32,16,3,2,128]{4,1,3,2,0:T(8,128)(2,1)S(1)} all-to-all(bf16[32,16,3,2,128]{4,1,3,2,0:T(8,128)(2,1)S(1)} %constant_dynamic-update-slice_fusion), channel_id=1, replica_groups=mesh['chan'=32,'stn'=8] {'chan'}, dimensions={0} | all-to-all | bytes 1572864 | tf_op jit(solution)/shard_map/all_to_all | solution.py:81
  200.7 1.2 copy.18
  202.0 0.1 constant_dynamic-slice_fusion
  202.4 0.1 reshape.30
  202.6 0.1 broadcast_in_dim.14
  202.7 0.2 copy.22
  202.9 1.2 fusion.59
  204.1 145.4 %all-gather.2.cloned.1.call-done = bf16[16,96,2,1024]{3,1,2,0:T(8,128)(2,1)} async-done(((bf16[16,96,2,128]{3,1,2,0:T(8,128)(2,1)}), bf16[16,96,2,1024]{3,1,2,0:T(8,128)(2,1)}) %all-gather.2.cloned.1.call-update) | async-done | bytes 6291472 | tf_op jit(solution)/shard_map/all_gather | solution.py:86
  349.5 1.3 dynamic-slice_dynamic-update-slice_fusion.4
  350.8 1.3 dynamic-slice_dynamic-update-slice_fusion.3
  352.1 1.3 dynamic-slice_dynamic-update-slice_fusion.2
  353.4 1.3 dynamic-slice_dynamic-update-slice_fusion.1
  354.8 1.3 dynamic-slice_dynamic-update-slice_fusion
  356.1 1.2 convolution_bitcast_fusion.1
  357.4 1.1 convolution_bitcast_fusion
  358.4 3.8 %fusion.1 = bf16[16,2,128,640]{3,2,0,1:T(8,128)(2,1)} fusion(f32[16,1,128,640]{3,2,0,1:T(8,128)S(1)} %convolution_bitcast_fusion, f32[16,1,128,640]{3,2,0,1:T(8,128)S(1)} %convolution_bitcast_fusion.1, f32[128,640]{1,0:T(8,128)S(1)} %copy.22), kind=kLoop, calls=%fused_computation.11 | loop fusion | flops 10485760 | bytes 16056320 | tf_op jit(solution)/shard_map/convert_element_type | solution.py:108
  362.2 5.6 %copy.23 = bf16[16,2,128,640]{3,2,1,0:T(8,128)(2,1)} copy(bf16[16,2,128,640]{3,2,0,1:T(8,128)(2,1)} %fusion.1) | data formatting | bytes 10485760 | tf_op jit(solution)/shard_map/convert_element_type | solution.py:108
  (49 shorter events, 0.7 us)
Async XLA Ops:
  6.5 12.5 %copy-start.1 = (s32[512]{0:T(512)S(1)}, s32[512]{0:T(512)}, u32[]{:S(2)}) copy-start(s32[512]{0:T(512)} %param.4) | copy-start | bytes 6148
  6.5 343.0 %all-gather.2.cloned.1.call-start = ((), (), s32[]{:S(2)}) async-start(), calls=%async_computation.1 | async-start | bytes 7077888 | tf_op jit(solution)/shard_map/all_gather | solution.py:86
  15.2 131.4 %collective-permute-start = (bf16[2,128,3,4096]{1,3,2,0:T(8,128)(2,1)}, bf16[2,128,3,4096]{1,3,2,0:T(8,128)(2,1)}, u32[]{:S(2)}, u32[]{:S(2)}) collective-permute-start(bf16[2,128,3,4096]{1,3,2,0:T(8,128)(2,1)} %bitcast.171), channel_id=1, source_target_pairs={{0,8},{8,16},{16,24},{24,32},{32,40},{40,48},{48,56},{56,64},{64,7... | collective-permute-start | bytes 18874376 | tf_op jit(solution)/shard_map/ppermute | solution.py:14
  51.1 95.5 %slice-start = ((s8[6291456]{0:T(1024)(128)(4,1)}), s8[4194304]{0:T(1024)(128)(4,1)S(1)}, s32[]{:S(2)}) async-start(s8[6291456]{0:T(1024)(128)(4,1)} %bitcast.172), calls=%async_computation.2 | async-start | bytes 8388608
  82.8 63.8 %slice-start.1 = ((s8[6291456]{0:T(1024)(128)(4,1)}), s8[2097152]{0:T(1024)(128)(4,1)S(1)}, s32[]{:S(2)}) async-start(s8[6291456]{0:T(1024)(128)(4,1)} %bitcast.172), calls=%async_computation.3 | async-start | bytes 4194304
  169.9 32.1 %copy-start = (s32[64,512]{1,0:T(8,128)S(1)}, s32[64,512]{1,0:T(8,128)}, u32[]{:S(2)}) copy-start(s32[64,512]{1,0:T(8,128)} %param.5) | copy-start | bytes 393220
Sparse Core Ops, SparseCore 0:
  202.1 147.4 all-gather.1
